TPU v7x, 256 devices: a whole 4x4x8 slice. The times are simulated.
256 devices in a mesh: quad: 4 (over x), box: 64 (over z, y, core).
Axes of the slice: x: 4, y: 4, z: 8, core: 2. Of those that a mesh axis runs over, the one named last changes fastest.
Arguments:
- sample_box: int32 [524288], P(('quad', 'box')), may hold values from -1 to 1023, as said below
- sample_coords: float32 [4, 524288], P(None, ('quad', 'box')), may hold values from -1 to 1
- sample_values: float32 [2, 524288], P(None, ('quad', 'box')), may hold values from -0.6 to 0.6
- level_one: float32 [2, 2, 128, 128], replicated, may hold values from -0.375 to 0.375
- level_two: float32 [2, 2, 128, 128], replicated, may hold values from -0.375 to 0.375
- phase_one: float32 [4, 1024, 64, 512], P('quad', 'box'), may hold values from -3.140625 to 3.140625
- phase_two: float32 [4, 1024, 64, 512], P('quad', 'box'), may hold values from -3.140625 to 3.140625
Outputs:
- image: float32 [4, 1024, 128, 512], P('quad', 'box')
Inputs may be any that keep to these rules, and one draw needn't show every extreme that they name: `sample_box`: rows of one device name boxes of that device's quadrant, or -1 for an empty row. Call owner o the boxes o * 16 to (o + 1) * 16 - 1. Among the rows of one device, each owner is named by 15 to 62 rows; one owner, the same for every device of a draw, is named by exactly 62 rows on every device.
All inputs are finite; a program needn't handle non-finite values.
Results may differ from a plain program's by a relative error of at most 0.0003.
Values sent between devices are 32-bit elements; how exact they have to be, the bound alone decides.
No kernel may reach another device: no remote copies, remote signals or barrier semaphores. Data moves between devices by JAX's collectives and lax.ppermute only.
A program may use at most 128 MiB of HBM per device.

v0:
```python
import jax
import jax.numpy as jnp
import numpy as np
from jax import lax
from jax.sharding import PartitionSpec as P

wavenumber = 6.0


def from_partner(value, axis, stride):
    mask = 2**stride
    pairs = [(source, source ^ mask) for source in range(lax.axis_size(axis))]
    return lax.ppermute(value, axis, pairs)


def node_table():
    nodes = np.cos(np.pi * (2.0 * np.arange(8) + 1.0) / 16.0)
    scales = []
    for center in range(8):
        product = 1.0
        for other_node in range(8):
            if other_node != center:
                product = product * (nodes[center] - nodes[other_node])
        scales.append(1.0 / product)
    return ([float(v) for v in nodes], scales)


def lagrange(points):
    nodes, scales = node_table()
    columns = []
    for center in range(8):
        factor = jnp.full_like(points, scales[center])
        for other_node in range(8):
            if other_node != center:
                factor = factor * (points - nodes[other_node])
        columns.append(factor)
    return jnp.stack(columns, axis=0)


def leaf_block(local_box, coords, values, box_count, targets):
    width = coords.shape[1]
    first_axis = lagrange(coords[0])
    second_axis = lagrange(coords[1])
    basis = (first_axis[:, None, :] * second_axis[None, :, :]).reshape(64, width)
    marks = (local_box[None, :] == jnp.arange(box_count, dtype=jnp.int32)[:, None]).astype(
        jnp.float32
    )
    weights = (marks[:, None, :] * basis[None, :, :]).reshape(box_count * 64, width)
    angles = 2.0 * jnp.pi * jnp.arange(targets, dtype=jnp.float32) / targets
    theta = wavenumber * (
        coords[2][None, :] * jnp.cos(angles)[:, None]
        + coords[3][None, :] * jnp.sin(angles)[:, None]
    )
    cosine = jnp.cos(theta)
    sine = jnp.sin(theta)
    real_part = values[0][None, :] * cosine - values[1][None, :] * sine
    imag_part = values[0][None, :] * sine + values[1][None, :] * cosine
    dims = (((1,), (1,)), ((), ()))
    real_sum = lax.dot_general(weights, real_part, dims, precision=lax.Precision.HIGHEST)
    imag_sum = lax.dot_general(weights, imag_part, dims, precision=lax.Precision.HIGHEST)
    stacked = jnp.stack(
        [real_sum.reshape(box_count, 64, targets), imag_sum.reshape(box_count, 64, targets)], axis=1
    )
    return stacked.reshape(box_count, 128, targets)


def apply_matrix(matrix, coef):
    return jnp.einsum("ij,bjt->bit", matrix, coef, precision=lax.Precision.HIGHEST)


def rotate(coef, angle):
    real_part = coef[:, :64]
    imag_part = coef[:, 64:]
    cosine = jnp.cos(angle)
    sine = jnp.sin(angle)
    return jnp.concatenate(
        [cosine * real_part - sine * imag_part, sine * real_part + cosine * imag_part], axis=1
    )


def evaluate(coef):
    pixels = -1.0 + (2.0 * jnp.arange(8, dtype=jnp.float32) + 1.0) / 8.0
    weights = lagrange(pixels)
    vmatrix = jnp.einsum("ki,mj->ijkm", weights, weights).reshape(64, 64)
    count = coef.shape[0]
    targets = coef.shape[2]
    parts = coef.reshape(count, 2, 64, targets)
    result = jnp.einsum("pj,bcjt->bcpt", vmatrix, parts, precision=lax.Precision.HIGHEST)
    return result.reshape(count, 128, targets)


def combine_pair(matrices, bit_value, own_coef, other_coef, angle):
    child_zero = jnp.where(bit_value == 0, own_coef, other_coef)
    child_one = jnp.where(bit_value == 0, other_coef, own_coef)
    summed = apply_matrix(matrices[0, bit_value], child_zero) + apply_matrix(
        matrices[1, bit_value], child_one
    )
    return rotate(summed, angle)


def body(sample_box, sample_coords, sample_values, level_one, level_two, phase_one, phase_two):
    owners_count = lax.axis_size("box")
    sample_rows = sample_box.shape[0]
    capacity = 2 * sample_rows // (owners_count + 2)
    box_count = phase_one.shape[1]
    targets = phase_one.shape[3]
    owner = jnp.where(sample_box >= 0, sample_box // box_count, owners_count)
    order = jnp.argsort(owner, stable=True)
    sorted_owner = owner[order]
    owner_ids = jnp.arange(owners_count, dtype=jnp.int32)
    starts = jnp.searchsorted(sorted_owner, owner_ids, side="left")
    stops = jnp.searchsorted(sorted_owner, owner_ids, side="right")
    local_box = (sample_box - owner * box_count).astype(jnp.float32)
    payload = jnp.concatenate([local_box[None, :], sample_coords, sample_values], axis=0)
    sorted_payload = payload[:, order]
    slot_ids = jnp.arange(capacity, dtype=jnp.int32)
    source_row = starts[:, None] + slot_ids[None, :]
    filled = source_row < stops[:, None]
    source_row = jnp.where(filled, source_row, 0).reshape(owners_count * capacity)
    packed = jnp.take(sorted_payload, source_row, axis=1).reshape(7, owners_count, capacity)
    packed = jnp.where(filled[None, :, :], packed, 0.0)
    arrived = lax.all_to_all(packed, "box", split_axis=1, concat_axis=1, tiled=True)
    group_size = 8

    def add_group(block_index, running):
        block = lax.dynamic_slice_in_dim(arrived, block_index * group_size, group_size, 1).reshape(
            7, group_size * capacity
        )
        return running + leaf_block(
            block[0].astype(jnp.int32), block[1:5], block[5:7], box_count, targets
        )

    leaf_coef = lax.fori_loop(
        0, owners_count // group_size, add_group, jnp.zeros((box_count, 128, targets), jnp.float32)
    )
    quad_index = lax.axis_index("quad")
    low_bit = quad_index % 2
    high_bit = quad_index // 2
    partner_leaf = from_partner(leaf_coef, "quad", 0)
    own_level = combine_pair(level_one, low_bit, leaf_coef, partner_leaf, phase_one[0])
    partner_level = from_partner(own_level, "quad", 1)
    final_coef = combine_pair(level_two, high_bit, own_level, partner_level, phase_two[0])
    return evaluate(final_coef)[None]


def solution(mesh):
    placed = (
        P(("quad", "box")),
        P(None, ("quad", "box")),
        P(None, ("quad", "box")),
        P(),
        P(),
        P("quad", "box", None, None),
        P("quad", "box", None, None),
    )
    return jax.shard_map(
        body, mesh=mesh, in_specs=placed, out_specs=P("quad", "box", None, None), check_vma=False
    )
```

profile of v0, /device:TPU:67, one launch (start us, length us, event | category | flops | bytes accessed | tf_op | source)
XLA Modules:
  0.0 508.7 jit_solution(13530832447084754221)
XLA Ops:
  5.8 11.8 %gather_fusion.2 = s32[2048]{0:T(1024)S(1)} fusion(s32[2048]{0:T(1024)S(1)} %get-tuple-element.391, s32[2048]{0:T(1024)S(1)} %fusion.89), kind=kCustom, calls=%fused_computation.2 | custom fusion | bytes 24576 | tf_op jit(solution)/shard_map/gather | solution.py:109
  17.6 9.9 %while.65 = (s32[]{:T(128)}, u32[64]{0:T(128)S(1)}, u32[64]{0:T(128)S(1)}, s32[2048]{0:T(1024)S(1)}, s32[]{:T(128)}, /*index=5*/s32[]{:T(128)}, s32[]{}) while((s32[]{:T(128)}, u32[64]{0:T(128)S(1)}, u32[64]{0:T(128)S(1)}, s32[2048]{0:T(1024)S(1)}, s32[]{:T(128)}, /*index=5*/s32[]{:T(128)}, s32[]{}) %tuple.134), condition=%wide.region_2.3_spmd.clone, body=%wide.region_1.2_spmd.clone.sunk | while | flops 1860 | bytes 7268 | solution.py:111
  27.8 9.9 %while.66 = (s32[]{:T(128)}, u32[64]{0:T(128)S(1)}, u32[64]{0:T(128)S(1)}, s32[2048]{0:T(1024)S(1)}, s32[]{:T(128)}, /*index=5*/s32[]{:T(128)}, s32[]{}) while((s32[]{:T(128)}, u32[64]{0:T(128)S(1)}, u32[64]{0:T(128)S(1)}, s32[2048]{0:T(1024)S(1)}, s32[]{:T(128)}, /*index=5*/s32[]{:T(128)}, s32[]{}) %tuple.143), condition=%wide.region_4.5_spmd.clone, body=%wide.region_3.4_spmd.clone.sunk | while | flops 1860 | bytes 7268 | solution.py:112
  52.7 11.6 %all-to-all-start = ((f32[64,1,434]{2,1,0:T(1,128)}), f32[64,1,434]{2,1,0:T(1,128)S(1)}, u32[]{:S(2)}, u32[]{:S(2)}) async-start(f32[64,1,434]{2,1,0:T(1,128)} %reshape.1860), calls=%async_computation | async-start | bytes 262144 | tf_op jit(solution)/shard_map/all_to_all | solution.py:122
  64.4 9.2 %all-to-all-done = f32[64,1,434]{2,1,0:T(1,128)S(1)} async-done(((f32[64,1,434]{2,1,0:T(1,128)}), f32[64,1,434]{2,1,0:T(1,128)S(1)}, u32[]{:S(2)}, u32[]{:S(2)}) %all-to-all-start) | async-done | bytes 111136 | tf_op jit(solution)/shard_map/all_to_all | solution.py:122
  75.2 213.3 %while.67 = (s32[]{:T(128)}, f32[16,128,512]{2,1,0:T(8,128)}, f32[7,64,62]{2,1,0:T(8,128)S(1)}, s32[]{:T(128)}, s32[]{:T(128)}, /*index=5*/s32[]{}, s32[]{:T(128...) while((s32[]{:T(128)}, f32[16,128,512]{2,1,0:T(8,128)}, f32[7,64,62]{2,1,0:T(8,128)S(1)}, ...), condition=%wide.region_6.7_spmd.clone, body=%wide.region_5.6_spmd.clone.sunk | while | flops 6248953344 | bytes 34295128 | solution.py:133
  77.7 7.5 %fusion.127 = f32[16,1,64,512]{3,2,0,1:T(8,128)S(1)} fusion(f32[64,496]{1,0:T(8,128)S(1)} %multiply_bitcast_fusion.3, f32[16,496]{1,0:T(8,128)S(1)} %fusion.124, f32[496]{0:T(512)S(1)} %mul.3428, f32[512]{0:T(512)S(1)} %get-tuple-element.521, f32[496]{0:T(512)S(1)} %mul.3429, f32[512]{0:T(512)S(1)} %get-tuple-element.523, f32[496]{0:T(512)S(1)} %mul.3430, ...), kind=kOutput, calls=%fused_computation.27.clone.1 | convolution fusion | flops 3122847744 | bytes 2267904 | tf_op jit(solution)/shard_map/while/body/eval_jaxpr/dot_general | solution.py:59
  85.1 7.4 %fusion.126 = f32[16,1,64,512]{3,2,0,1:T(8,128)S(1)} fusion(f32[64,496]{1,0:T(8,128)S(1)} %multiply_bitcast_fusion.3, f32[16,496]{1,0:T(8,128)S(1)} %fusion.124, f32[496]{0:T(512)S(1)} %mul.3428, f32[512]{0:T(512)S(1)} %get-tuple-element.521, f32[496]{0:T(512)S(1)} %mul.3429, f32[512]{0:T(512)S(1)} %get-tuple-element.523, f32[496]{0:T(512)S(1)} %mul.3430, ...), kind=kOutput, calls=%fused_computation.28.clone.1 | convolution fusion | flops 3122847744 | bytes 2267904 | tf_op jit(solution)/shard_map/while/body/eval_jaxpr/dot_general | solution.py:60
  103.1 7.5 %fusion.127 = f32[16,1,64,512]{3,2,0,1:T(8,128)S(1)} fusion(f32[64,496]{1,0:T(8,128)S(1)} %multiply_bitcast_fusion.3, f32[16,496]{1,0:T(8,128)S(1)} %fusion.124, f32[496]{0:T(512)S(1)} %mul.3428, f32[512]{0:T(512)S(1)} %get-tuple-element.521, f32[496]{0:T(512)S(1)} %mul.3429, f32[512]{0:T(512)S(1)} %get-tuple-element.523, f32[496]{0:T(512)S(1)} %mul.3430, ...), kind=kOutput, calls=%fused_computation.27.clone.1 | convolution fusion | flops 3122847744 | bytes 2267904 | tf_op jit(solution)/shard_map/while/body/eval_jaxpr/dot_general | solution.py:59
  129.9 7.5 %fusion.127 = f32[16,1,64,512]{3,2,0,1:T(8,128)S(1)} fusion(f32[64,496]{1,0:T(8,128)S(1)} %multiply_bitcast_fusion.3, f32[16,496]{1,0:T(8,128)S(1)} %fusion.124, f32[496]{0:T(512)S(1)} %mul.3428, f32[512]{0:T(512)S(1)} %get-tuple-element.521, f32[496]{0:T(512)S(1)} %mul.3429, f32[512]{0:T(512)S(1)} %get-tuple-element.523, f32[496]{0:T(512)S(1)} %mul.3430, ...), kind=kOutput, calls=%fused_computation.27.clone.1 | convolution fusion | flops 3122847744 | bytes 2267904 | tf_op jit(solution)/shard_map/while/body/eval_jaxpr/dot_general | solution.py:59
  137.3 7.4 %fusion.126 = f32[16,1,64,512]{3,2,0,1:T(8,128)S(1)} fusion(f32[64,496]{1,0:T(8,128)S(1)} %multiply_bitcast_fusion.3, f32[16,496]{1,0:T(8,128)S(1)} %fusion.124, f32[496]{0:T(512)S(1)} %mul.3428, f32[512]{0:T(512)S(1)} %get-tuple-element.521, f32[496]{0:T(512)S(1)} %mul.3429, f32[512]{0:T(512)S(1)} %get-tuple-element.523, f32[496]{0:T(512)S(1)} %mul.3430, ...), kind=kOutput, calls=%fused_computation.28.clone.1 | convolution fusion | flops 3122847744 | bytes 2267904 | tf_op jit(solution)/shard_map/while/body/eval_jaxpr/dot_general | solution.py:60
  156.6 7.5 %fusion.127 = f32[16,1,64,512]{3,2,0,1:T(8,128)S(1)} fusion(f32[64,496]{1,0:T(8,128)S(1)} %multiply_bitcast_fusion.3, f32[16,496]{1,0:T(8,128)S(1)} %fusion.124, f32[496]{0:T(512)S(1)} %mul.3428, f32[512]{0:T(512)S(1)} %get-tuple-element.521, f32[496]{0:T(512)S(1)} %mul.3429, f32[512]{0:T(512)S(1)} %get-tuple-element.523, f32[496]{0:T(512)S(1)} %mul.3430, ...), kind=kOutput, calls=%fused_computation.27.clone.1 | convolution fusion | flops 3122847744 | bytes 2267904 | tf_op jit(solution)/shard_map/while/body/eval_jaxpr/dot_general | solution.py:59
  164.1 7.4 %fusion.126 = f32[16,1,64,512]{3,2,0,1:T(8,128)S(1)} fusion(f32[64,496]{1,0:T(8,128)S(1)} %multiply_bitcast_fusion.3, f32[16,496]{1,0:T(8,128)S(1)} %fusion.124, f32[496]{0:T(512)S(1)} %mul.3428, f32[512]{0:T(512)S(1)} %get-tuple-element.521, f32[496]{0:T(512)S(1)} %mul.3429, f32[512]{0:T(512)S(1)} %get-tuple-element.523, f32[496]{0:T(512)S(1)} %mul.3430, ...), kind=kOutput, calls=%fused_computation.28.clone.1 | convolution fusion | flops 3122847744 | bytes 2267904 | tf_op jit(solution)/shard_map/while/body/eval_jaxpr/dot_general | solution.py:60
  183.4 7.5 %fusion.127 = f32[16,1,64,512]{3,2,0,1:T(8,128)S(1)} fusion(f32[64,496]{1,0:T(8,128)S(1)} %multiply_bitcast_fusion.3, f32[16,496]{1,0:T(8,128)S(1)} %fusion.124, f32[496]{0:T(512)S(1)} %mul.3428, f32[512]{0:T(512)S(1)} %get-tuple-element.521, f32[496]{0:T(512)S(1)} %mul.3429, f32[512]{0:T(512)S(1)} %get-tuple-element.523, f32[496]{0:T(512)S(1)} %mul.3430, ...), kind=kOutput, calls=%fused_computation.27.clone.1 | convolution fusion | flops 3122847744 | bytes 2267904 | tf_op jit(solution)/shard_map/while/body/eval_jaxpr/dot_general | solution.py:59
  190.8 7.4 %fusion.126 = f32[16,1,64,512]{3,2,0,1:T(8,128)S(1)} fusion(f32[64,496]{1,0:T(8,128)S(1)} %multiply_bitcast_fusion.3, f32[16,496]{1,0:T(8,128)S(1)} %fusion.124, f32[496]{0:T(512)S(1)} %mul.3428, f32[512]{0:T(512)S(1)} %get-tuple-element.521, f32[496]{0:T(512)S(1)} %mul.3429, f32[512]{0:T(512)S(1)} %get-tuple-element.523, f32[496]{0:T(512)S(1)} %mul.3430, ...), kind=kOutput, calls=%fused_computation.28.clone.1 | convolution fusion | flops 3122847744 | bytes 2267904 | tf_op jit(solution)/shard_map/while/body/eval_jaxpr/dot_general | solution.py:60
  210.1 7.5 %fusion.127 = f32[16,1,64,512]{3,2,0,1:T(8,128)S(1)} fusion(f32[64,496]{1,0:T(8,128)S(1)} %multiply_bitcast_fusion.3, f32[16,496]{1,0:T(8,128)S(1)} %fusion.124, f32[496]{0:T(512)S(1)} %mul.3428, f32[512]{0:T(512)S(1)} %get-tuple-element.521, f32[496]{0:T(512)S(1)} %mul.3429, f32[512]{0:T(512)S(1)} %get-tuple-element.523, f32[496]{0:T(512)S(1)} %mul.3430, ...), kind=kOutput, calls=%fused_computation.27.clone.1 | convolution fusion | flops 3122847744 | bytes 2267904 | tf_op jit(solution)/shard_map/while/body/eval_jaxpr/dot_general | solution.py:59
  236.8 7.5 %fusion.127 = f32[16,1,64,512]{3,2,0,1:T(8,128)S(1)} fusion(f32[64,496]{1,0:T(8,128)S(1)} %multiply_bitcast_fusion.3, f32[16,496]{1,0:T(8,128)S(1)} %fusion.124, f32[496]{0:T(512)S(1)} %mul.3428, f32[512]{0:T(512)S(1)} %get-tuple-element.521, f32[496]{0:T(512)S(1)} %mul.3429, f32[512]{0:T(512)S(1)} %get-tuple-element.523, f32[496]{0:T(512)S(1)} %mul.3430, ...), kind=kOutput, calls=%fused_computation.27.clone.1 | convolution fusion | flops 3122847744 | bytes 2267904 | tf_op jit(solution)/shard_map/while/body/eval_jaxpr/dot_general | solution.py:59
  244.3 7.4 %fusion.126 = f32[16,1,64,512]{3,2,0,1:T(8,128)S(1)} fusion(f32[64,496]{1,0:T(8,128)S(1)} %multiply_bitcast_fusion.3, f32[16,496]{1,0:T(8,128)S(1)} %fusion.124, f32[496]{0:T(512)S(1)} %mul.3428, f32[512]{0:T(512)S(1)} %get-tuple-element.521, f32[496]{0:T(512)S(1)} %mul.3429, f32[512]{0:T(512)S(1)} %get-tuple-element.523, f32[496]{0:T(512)S(1)} %mul.3430, ...), kind=kOutput, calls=%fused_computation.28.clone.1 | convolution fusion | flops 3122847744 | bytes 2267904 | tf_op jit(solution)/shard_map/while/body/eval_jaxpr/dot_general | solution.py:60
  263.6 7.5 %fusion.127 = f32[16,1,64,512]{3,2,0,1:T(8,128)S(1)} fusion(f32[64,496]{1,0:T(8,128)S(1)} %multiply_bitcast_fusion.3, f32[16,496]{1,0:T(8,128)S(1)} %fusion.124, f32[496]{0:T(512)S(1)} %mul.3428, f32[512]{0:T(512)S(1)} %get-tuple-element.521, f32[496]{0:T(512)S(1)} %mul.3429, f32[512]{0:T(512)S(1)} %get-tuple-element.523, f32[496]{0:T(512)S(1)} %mul.3430, ...), kind=kOutput, calls=%fused_computation.27.clone.1 | convolution fusion | flops 3122847744 | bytes 2267904 | tf_op jit(solution)/shard_map/while/body/eval_jaxpr/dot_general | solution.py:59
  271.1 7.4 %fusion.126 = f32[16,1,64,512]{3,2,0,1:T(8,128)S(1)} fusion(f32[64,496]{1,0:T(8,128)S(1)} %multiply_bitcast_fusion.3, f32[16,496]{1,0:T(8,128)S(1)} %fusion.124, f32[496]{0:T(512)S(1)} %mul.3428, f32[512]{0:T(512)S(1)} %get-tuple-element.521, f32[496]{0:T(512)S(1)} %mul.3429, f32[512]{0:T(512)S(1)} %get-tuple-element.523, f32[496]{0:T(512)S(1)} %mul.3430, ...), kind=kOutput, calls=%fused_computation.28.clone.1 | convolution fusion | flops 3122847744 | bytes 2267904 | tf_op jit(solution)/shard_map/while/body/eval_jaxpr/dot_general | solution.py:60
  296.2 84.1 %collective-permute-done = f32[16,128,512]{2,1,0:T(8,128)} collective-permute-done((f32[16,128,512]{2,1,0:T(8,128)}, f32[16,128,512]{2,1,0:T(8,128)}, u32[]{:S(2)}, u32[]{:S(2)}) %collective-permute-start) | collective-permute-done | bytes 4194336 | tf_op jit(solution)/shard_map/ppermute | solution.py:13
  385.2 7.7 %add_bitcast_fusion.1 = f32[16,128,512]{2,1,0:T(8,128)S(1)} fusion(f32[16,512,128]{1,2,0:T(8,128)S(1)} %fusion.59, f32[16,128,512]{2,1,0:T(8,128)S(1)} %copy-done.1, f32[16,128,512]{2,1,0:T(8,128)} %collective-permute-done, pred[]{:T(512)S(6)} %eq.48, f32[2,2,128,128]{3,2,1,0:T(8,128)S(1)} %copy-done, s32[]{:T(128)S(6)} %select_n.146), kind=kOutput, calls=%fused_computation.96 | convolution fusion | flops 1612709888 | bytes 16842756 | tf_op jit(solution)/shard_map/ij,bjt->bit/dot_general | solution.py:68
  399.0 8.7 %fusion.106 = (f32[1,16,64,512]{3,2,1,0:T(8,128)S(1)}, f32[1,16,64,512]{3,2,1,0:T(8,128)S(1)}) fusion(f32[1,16,64,512]{3,2,1,0:T(8,128)} %param.19), kind=kLoop, calls=%fused_computation.173 | loop fusion | bytes 6291456 | tf_op jit(solution)/shard_map/cos | solution.py:74
  407.7 81.3 %collective-permute-done.1 = f32[16,128,512]{2,1,0:T(8,128)} collective-permute-done((f32[16,128,512]{2,1,0:T(8,128)}, f32[16,128,512]{2,1,0:T(8,128)}, u32[]{:S(2)}, u32[]{:S(2)}) %collective-permute-start.1) | collective-permute-done | bytes 4194336 | tf_op jit(solution)/shard_map/ppermute | solution.py:13
  (403 shorter events, 187.5 us)
Async XLA Ops:
  0.0 380.3 %copy-start = (f32[2,2,128,128]{3,2,1,0:T(8,128)S(1)}, f32[2,2,128,128]{3,2,1,0:T(8,128)}, u32[]{:S(2)}) copy-start(f32[2,2,128,128]{3,2,1,0:T(8,128)} %param.16) | copy-start | bytes 786436
  17.6 20.5 %copy-start.6 = (f32[4,2048]{1,0:T(4,128)S(1)}, f32[4,2048]{1,0:T(4,128)}, u32[]{:S(2)}) copy-start(f32[4,2048]{1,0:T(4,128)} %param.14) | copy-start | bytes 98308
  17.6 20.5 %copy-start.7 = (f32[2,2048]{1,0:T(2,128)S(1)}, f32[2,2048]{1,0:T(2,128)}, u32[]{:S(2)}) copy-start(f32[2,2048]{1,0:T(2,128)} %param.15) | copy-start | bytes 49156
  52.7 20.8 %all-to-all-start = ((f32[64,1,434]{2,1,0:T(1,128)}), f32[64,1,434]{2,1,0:T(1,128)S(1)}, u32[]{:S(2)}, u32[]{:S(2)}) async-start(f32[64,1,434]{2,1,0:T(1,128)} %reshape.1860), calls=%async_computation | async-start | bytes 262144 | tf_op jit(solution)/shard_map/all_to_all | solution.py:122
  75.2 213.7 %copy-start.4 = (f32[1,16,64,512]{3,2,1,0:T(8,128)S(1)}, f32[1,16,64,512]{3,2,1,0:T(8,128)}, u32[]{:S(2)}) copy-start(f32[1,16,64,512]{3,2,1,0:T(8,128)} %param.18) | copy-start | bytes 6291460
  288.6 91.7 %collective-permute-start = (f32[16,128,512]{2,1,0:T(8,128)}, f32[16,128,512]{2,1,0:T(8,128)}, u32[]{:S(2)}, u32[]{:S(2)}) collective-permute-start(f32[16,128,512]{2,1,0:T(8,128)} %get-tuple-element.284), channel_id=1, source_target_pairs={{0,64},{64,0},{128,192},{192,128},{1,65},{65,1},{129,193},{193,129... | collective-permute-start | bytes 12582920 | tf_op jit(solution)/shard_map/ppermute | solution.py:13
  288.9 91.4 %copy-start.1 = (f32[16,128,512]{2,1,0:T(8,128)S(1)}, f32[16,128,512]{2,1,0:T(8,128)}, u32[]{:S(2)}) copy-start(f32[16,128,512]{2,1,0:T(8,128)} %get-tuple-element.284) | copy-start | bytes 12582916
  394.0 2.7 copy-start.2
  396.8 92.2 %copy-start.5 = (f32[2,2,128,128]{3,2,1,0:T(8,128)S(1)}, f32[2,2,128,128]{3,2,1,0:T(8,128)}, u32[]{:S(2)}) copy-start(f32[2,2,128,128]{3,2,1,0:T(8,128)} %param.17) | copy-start | bytes 786436
  396.8 92.2 %collective-permute-start.1 = (f32[16,128,512]{2,1,0:T(8,128)}, f32[16,128,512]{2,1,0:T(8,128)}, u32[]{:S(2)}, u32[]{:S(2)}) collective-permute-start(f32[16,128,512]{2,1,0:T(8,128)} %pad_maximum_fusion.1), channel_id=1, source_target_pairs={{0,128},{64,192},{128,0},{192,64},{1,129},{65,193},{129,1},{193,65... | collective-permute-start | bytes 12582920 | tf_op jit(solution)/shard_map/ppermute | solution.py:13
  399.0 90.0 %copy-start.3 = (f32[16,64,512]{2,1,0:T(8,128)S(1)}, f32[16,64,512]{2,1,0:T(8,128)}, u32[]{:S(2)}) copy-start(f32[16,64,512]{2,1,0:T(8,128)} %copy-done.2) | copy-start | bytes 6291460
where the time goes:
time: 518 us; the launch traced here: 509 us
  waiting for transfers between devices  175 us (34%)
  matrix products  150 us (29%)
  local copies, waits for them, and re-layouts  96.4 us (19%)
  other arithmetic  71.8 us (14%)
  starting transfers between devices  13.8 us (3%)
    ppermute x2, waiting for transfers between devices, from_partner(): return lax.ppermute(value, axis, pairs)  165 us
    dot_general x8, matrix products, leaf_block(): lax.dot_general(weights, real_part, dims, precision=lax.Precision.HIGHEST)  59.7 us
    dot_general x8, matrix products, leaf_block(): lax.dot_general(weights, imag_part, dims, precision=lax.Precision.HIGHEST)  59.5 us
    add x8, other arithmetic, add_group(): running + leaf_block(block[0].astype(jnp.int32), block[1:5], block[5:7],...  52.1 us
    dot_general x4, matrix products, apply_matrix(): jnp.einsum('ij,bjt->bit', matrix, coef, precision=lax.Precision.HIGHEST)  25.2 us
    another operation x8, local copies, waits for them, and re-layouts, leaf_block(): jnp.stack([real_sum.reshape(box_count, 64, targets), imag_sum.reshape(box...  20.2 us
    cos x2, local copies, waits for them, and re-layouts, rotate(): cosine = jnp.cos(angle)  16 us
    gather x1, local copies, waits for them, and re-layouts, body(): sorted_owner = owner[order]  11.8 us
  transfers between devices with their start and end apart: 3, of which 3 were waited for; matrix products, arithmetic and copies ran while one was open for 3% of the time, Pallas kernels for 0%

commit v1 on v0

v1 whole, which is shorter than its diff:
```python
import functools

import jax
import jax.numpy as jnp
import numpy as np
from jax import lax
from jax.experimental import pallas as pl
from jax.experimental.pallas import tpu as pltpu
from jax.sharding import PartitionSpec as P

WAVENUMBER = 6.0
SLOTS = 64
TILE = 256
VMEM_LIMIT = 56 * 1024 * 1024

F32 = jnp.float32
BF16 = jnp.bfloat16
NN = (((1,), (0,)), ((), ()))
NT = (((1,), (1,)), ((), ()))


def node_table():
    nodes = np.cos(np.pi * (2.0 * np.arange(8) + 1.0) / 16.0)
    scales = []
    for center in range(8):
        product = 1.0
        for other_node in range(8):
            if other_node != center:
                product = product * (nodes[center] - nodes[other_node])
        scales.append(1.0 / product)
    return ([float(v) for v in nodes], scales)


def lagrange_row(points, center):
    nodes, scales = node_table()
    factor = None
    for other_node in range(8):
        if other_node != center:
            term = points - nodes[other_node]
            factor = term if factor is None else factor * term
    return factor * scales[center]


def pixel_matrix():
    nodes, scales = node_table()
    pixels = -1.0 + (2.0 * np.arange(8) + 1.0) / 8.0
    weights = np.zeros((8, 8))
    for center in range(8):
        value = np.full(8, scales[center])
        for other_node in range(8):
            if other_node != center:
                value = value * (pixels - nodes[other_node])
        weights[center] = value
    one_part = np.einsum("ki,mj->ijkm", weights, weights).reshape(64, 64)
    return np.kron(np.eye(2), one_part).astype(np.float32)


def series(function, limit, terms):
    grid = 0.5 * limit * limit * (1.0 - np.cos(np.pi * (np.arange(400) + 0.5) / 400))
    values = function(np.sqrt(grid))
    fit = np.polynomial.chebyshev.Chebyshev.fit(grid, values, terms - 1, domain=[0, limit * limit])
    return [float(v) for v in fit.convert(kind=np.polynomial.Polynomial).coef]


def horner(coefs, square):
    total = coefs[-1]
    for coef in coefs[-2::-1]:
        total = total * square + coef
    return total


def cos_sin(small, doublings, limit, sin_terms, cos_terms):
    square = small * small
    sine = horner(series(lambda x: np.sinc(x / np.pi), limit, sin_terms), square) * small
    cosine = horner(series(np.cos, limit, cos_terms), square)
    for _ in range(doublings):
        twice = sine + sine
        cosine, sine = 1.0 - twice * sine, twice * cosine
    return cosine, sine


def split_two(value):
    high = value.astype(BF16)
    return high, (value - high.astype(F32)).astype(BF16)


def split_three(value):
    high = value.astype(BF16)
    rest = value - high.astype(F32)
    middle = rest.astype(BF16)
    low = (rest - middle.astype(F32)).astype(BF16)
    return high, middle, low


def product(left, right, dims=NN):
    left_high, left_low = split_two(left)
    right_high, right_low = split_two(right)
    dot = functools.partial(lax.dot_general, dimension_numbers=dims, preferred_element_type=F32)
    return dot(left_high, right_high) + (dot(left_low, right_high) + dot(left_high, right_low))


def strict_upper(size):
    rows = lax.broadcasted_iota(jnp.int32, (size, size), 0)
    columns = lax.broadcasted_iota(jnp.int32, (size, size), 1)
    return jnp.where(rows < columns, 1.0, 0.0).astype(BF16)


def pack_kernel(box_ref, coords_ref, values_ref, out_ref):
    owners = out_ref.shape[0] // 4
    rows = box_ref.shape[1]
    tri = strict_upper(256)
    owner_ids = lax.broadcasted_iota(jnp.int32, (owners, 256), 0)
    row_owner = lax.broadcasted_iota(jnp.int32, (owners * 4, 256), 0) >> 2
    slot_ids = lax.broadcasted_iota(jnp.int32, (2 * SLOTS, 256), 0)
    carry = jnp.zeros((owners, 1), F32)
    total = jnp.zeros((owners * 4, 2 * SLOTS), F32)
    for start in range(0, rows, 256):
        box = box_ref[:, start : start + 256]
        owner = box >> 4
        mark = jnp.where(owner_ids == owner, 1.0, 0.0)
        ahead = lax.dot_general(mark.astype(BF16), tri, NN, preferred_element_type=F32) + carry
        carry = carry + jnp.sum(mark, axis=1, keepdims=True)
        slot = jnp.sum(mark * ahead, axis=0, keepdims=True).astype(jnp.int32)
        key = ((box & 15) + 1).astype(F32)
        coords = coords_ref[:, start : start + 256]
        values = values_ref[:, start : start + 256]
        empty = jnp.zeros_like(key)
        low_fields = jnp.concatenate([key, coords[0:3]], axis=0)
        high_fields = jnp.concatenate([coords[3:4], values, empty], axis=0)
        hit = row_owner == owner
        for fields, shift in ((low_fields, 0), (high_fields, SLOTS)):
            place = jnp.where(slot_ids == slot + shift, 1.0, 0.0).astype(BF16)
            twice = jnp.concatenate([fields, fields], axis=0)
            spread = jnp.broadcast_to(twice[None], (owners // 2, 8, 256)).reshape(owners * 4, 256)
            for part in split_three(jnp.where(hit, spread, 0.0)):
                total = total + lax.dot_general(part, place, NT, preferred_element_type=F32)
    out_ref[...] = total


def sort_kernel(in_ref, out_ref, fields_ref):
    senders = in_ref.shape[0] // 4
    tiles = senders * SLOTS // 128
    lane = lax.broadcasted_iota(jnp.int32, (4, 128), 1)
    for pair in range(senders // 2):
        first = in_ref[8 * pair : 8 * pair + 4, :]
        second = in_ref[8 * pair + 4 : 8 * pair + 8, :]
        low = jnp.where(lane < SLOTS, first, pltpu.roll(second, SLOTS, 1))
        high = jnp.where(lane < SLOTS, pltpu.roll(first, SLOTS, 1), second)
        fields_ref[:, 128 * pair : 128 * (pair + 1)] = jnp.concatenate([low, high], axis=0)
    width = tiles * 128
    tri = strict_upper(256)
    ids = lax.broadcasted_iota(jnp.int32, (16, 256), 0) + 1
    base = jnp.zeros((16, 1), F32)
    count = jnp.zeros((1, 1), F32)
    for start in range(0, width, 256):
        key = fields_ref[0:1, start : start + 256].astype(jnp.int32)
        below = (key >= 1) & (key < ids)
        base = base + jnp.sum(jnp.where(below, 1.0, 0.0), axis=1, keepdims=True)
        count = count + jnp.sum(jnp.where(key >= 1, 1.0, 0.0), axis=1, keepdims=True)
    tile_ids = lax.broadcasted_iota(jnp.int32, (tiles * 8, 256), 0) >> 3
    lane_ids = lax.broadcasted_iota(jnp.int32, (128, 256), 0)
    carry = base
    total = jnp.zeros((tiles * 8, 128), F32)
    for start in range(0, width, 256):
        fields = fields_ref[:, start : start + 256]
        key = fields[0:1].astype(jnp.int32)
        mark = jnp.where(key == ids, 1.0, 0.0)
        ahead = lax.dot_general(mark.astype(BF16), tri, NN, preferred_element_type=F32) + carry
        carry = carry + jnp.sum(mark, axis=1, keepdims=True)
        spot = jnp.sum(mark * ahead, axis=0, keepdims=True).astype(jnp.int32)
        spot = jnp.where(key >= 1, spot, -1)
        hit = tile_ids == (spot >> 7)
        place = jnp.where(lane_ids == (spot & 127), 1.0, 0.0).astype(BF16)
        spread = jnp.broadcast_to(fields[None], (tiles, 8, 256)).reshape(tiles * 8, 256)
        for part in split_three(jnp.where(hit, spread, 0.0)):
            total = total + lax.dot_general(part, place, NT, preferred_element_type=F32)
    out_ref[0:tiles] = total.reshape(tiles, 8, 128)
    out_ref[tiles] = jnp.broadcast_to(base[0:8], (8, 128))
    out_ref[tiles + 1] = jnp.broadcast_to(base[8:16], (8, 128))
    out_ref[tiles + 2] = jnp.broadcast_to(count, (8, 128))


def leaf_kernel(
    info_ref, s0_ref, s1_ref, s2_ref, s3_ref, circle_ref, one_ref, two_ref, phase_ref,
    partner_ref, own_ref, fields_ref, wave_ref, weight_ref, leaf_ref, state_ref,
):
    box = pl.program_id(0)
    tiles = s0_ref.shape[0] - 3

    @pl.when(box == 0)
    def _():
        for index, ref in enumerate((s0_ref, s1_ref, s2_ref, s3_ref)):
            for tile in range(tiles):
                fields_ref[index, tile // 2, :, 128 * (tile % 2) : 128 * (tile % 2 + 1)] = ref[tile]
            state_ref[index] = -1

    @pl.loop(0, 4)
    def _(index):
        start = info_ref[index, box]
        stop = info_ref[index, box + 1]
        leaf_ref[index] = jnp.zeros_like(leaf_ref[index])

        @pl.loop(start // TILE, (stop + TILE - 1) // TILE)
        def _(tile):
            @pl.when(state_ref[index] != tile)
            def _():
                state_ref[index] = tile
                fields = fields_ref[index, tile]
                for half in range(2):
                    columns = slice(128 * half, 128 * (half + 1))
                    first = fields[3:4, columns]
                    second = fields[4:5, columns]
                    for row in range(0, 256, 32):
                        small = (
                            circle_ref[0, row : row + 32] * first
                            + circle_ref[1, row : row + 32] * second
                        )
                        cosine, sine = cos_sin(small, 3, 1.0608, 4, 5)
                        for part, value in ((0, cosine), (256, sine)):
                            high, low = split_two(value)
                            wave_ref[index, 0, part + row : part + row + 32, columns] = high
                            wave_ref[index, 1, part + row : part + row + 32, columns] = low
                first_axis = [lagrange_row(fields[1:2], k) for k in range(8)]
                second_axis = jnp.concatenate(
                    [lagrange_row(fields[2:3], k) for k in range(8)], axis=0
                )
                for part in range(2):
                    scaled = second_axis * fields[5 + part : 6 + part]
                    weights = jnp.concatenate([first_axis[k] * scaled for k in range(8)], axis=0)
                    high, low = split_two(weights)
                    weight_ref[index, 64 * part : 64 * part + 64] = high
                    weight_ref[index, 128 + 64 * part : 192 + 64 * part] = low

            key = fields_ref[index, tile, 0:1, :].astype(jnp.int32)
            inside = jnp.broadcast_to(jnp.where(key == box + 1, 1.0, 0.0), (256, TILE)).astype(BF16)
            weights = weight_ref[index] * inside
            both = lax.dot_general(weights, wave_ref[index, 0], NT, preferred_element_type=F32)
            rest = lax.dot_general(
                weights[0:128], wave_ref[index, 1], NT, preferred_element_type=F32
            )
            leaf_ref[index] += both[0:128] + (both[128:256] + rest)

    low_bit = info_ref[4, 0]
    high_bit = info_ref[4, 1]
    matrix = jnp.concatenate([one_ref[low_bit, low_bit], one_ref[1 - low_bit, low_bit]], axis=1)

    def first_level(index):
        parts = []
        for child in (index, index + 1):
            real_cos = leaf_ref[child, 0:64, 0:256]
            real_sin = leaf_ref[child, 0:64, 256:512]
            imag_cos = leaf_ref[child, 64:128, 0:256]
            imag_sin = leaf_ref[child, 64:128, 256:512]
            parts.append(jnp.concatenate([real_cos - imag_sin, real_cos + imag_sin], axis=1))
            parts.append(jnp.concatenate([real_sin + imag_cos, imag_cos - real_sin], axis=1))
        return product(matrix, jnp.concatenate(parts, axis=0))

    partner_ref[0] = first_level(2)
    own = rotate(first_level(0), phase_ref[0])
    own_ref[0] = product(two_ref[high_bit, high_bit], own)


def rotate(coef, angle):
    cosine, sine = cos_sin(angle * 0.5, 1, 1.5708, 5, 6)
    real_part = coef[:64]
    imag_part = coef[64:]
    return jnp.concatenate(
        [cosine * real_part - sine * imag_part, sine * real_part + cosine * imag_part], axis=0
    )


def image_kernel(info_ref, partner_ref, own_ref, one_ref, two_ref, matrix_ref, pixel_ref, *rest):
    out_ref = rest[-1]
    high_bit = info_ref[4, 1]
    first = rotate(partner_ref[0], one_ref[0])
    second = own_ref[0] + product(matrix_ref[1 - high_bit, high_bit], first)
    out_ref[0] = product(pixel_ref[...], rotate(second, two_ref[0]))


def whole(shape):
    return pl.BlockSpec(shape, lambda *_: (0,) * len(shape))


def params():
    return pltpu.CompilerParams(vmem_limit_bytes=VMEM_LIMIT)


def from_quad(value, mask):
    pairs = [(source, source ^ mask) for source in range(lax.axis_size("quad"))]
    return lax.ppermute(value, "quad", pairs)


def image_part(info, partner, own, partner_phase, phase_two, level_two, pixel, done, begin):
    boxes, _, targets = own.shape
    count = partner_phase.shape[0]

    def moved(height):
        return pl.BlockSpec((1, height, targets), lambda b, *_: (b + begin, 0, 0))

    in_specs = [
        moved(128),
        moved(128),
        pl.BlockSpec((1, 64, targets), lambda b, *_: (b, 0, 0)),
        moved(64),
        whole(level_two.shape),
        whole(pixel.shape),
    ]
    operands = [partner, own, partner_phase, phase_two, level_two, pixel]
    aliases = {}
    if done is not None:
        in_specs.append(pl.BlockSpec(memory_space=pl.ANY))
        operands.append(done)
        aliases = {len(operands): 0}
    return pl.pallas_call(
        image_kernel,
        grid_spec=pltpu.PrefetchScalarGridSpec(
            num_scalar_prefetch=1, grid=(count,), in_specs=in_specs, out_specs=moved(128)
        ),
        out_shape=jax.ShapeDtypeStruct((boxes, 128, targets), F32),
        input_output_aliases=aliases,
        compiler_params=params(),
        name="image_part",
    )(info, *operands)


def body(sample_box, sample_coords, sample_values, level_one, level_two, phase_one, phase_two):
    senders = lax.axis_size("box")
    boxes = phase_one.shape[1]
    targets = phase_one.shape[3]
    tiles = senders * SLOTS // 128
    half = boxes // 2
    phase_one = phase_one[0]
    phase_two = phase_two[0]

    early_phase = from_quad(phase_one[:half], 2)

    packed = pl.pallas_call(
        pack_kernel,
        out_shape=jax.ShapeDtypeStruct((senders * 4, 128), F32),
        compiler_params=params(),
        name="pack",
    )(sample_box.reshape(1, -1), sample_coords, sample_values)
    arrived = lax.all_to_all(
        packed.reshape(senders, 4, 128), "box", split_axis=0, concat_axis=0, tiled=True
    )
    ordered = pl.pallas_call(
        sort_kernel,
        out_shape=jax.ShapeDtypeStruct((tiles + 3, 8, 128), F32),
        scratch_shapes=[pltpu.VMEM((8, tiles * 128), F32)],
        compiler_params=params(),
        name="sort",
    )(arrived.reshape(senders * 4, 128))
    groups = [ordered] + [from_quad(ordered, mask) for mask in (1, 2, 3)]
    late_source, _ = lax.optimization_barrier((phase_one[half:], ordered))
    late_phase = from_quad(late_source, 2)

    quad_index = lax.axis_index("quad")
    bits = jnp.zeros((24,), jnp.int32).at[0].set(quad_index % 2).at[1].set(quad_index // 2)
    starts = [group[tiles:, :, 0].reshape(24).astype(jnp.int32) for group in groups]
    info = jnp.stack(starts + [bits], axis=0)

    angles = 2.0 * np.pi * np.arange(256) / targets
    circle = np.stack([np.cos(angles), np.sin(angles)]) * (WAVENUMBER / 8.0)
    circle = jnp.asarray(np.repeat(circle[:, :, None], 128, axis=2), F32)

    def moved(height):
        return pl.BlockSpec((1, height, targets), lambda b, *_: (b, 0, 0))

    partner, own = pl.pallas_call(
        leaf_kernel,
        grid_spec=pltpu.PrefetchScalarGridSpec(
            num_scalar_prefetch=1,
            grid=(boxes,),
            in_specs=[whole(ordered.shape)] * 4
            + [whole(circle.shape), whole(level_one.shape), whole(level_two.shape), moved(64)],
            out_specs=[moved(128), moved(128)],
            scratch_shapes=[
                pltpu.VMEM((4, tiles // 2, 8, TILE), F32),
                pltpu.VMEM((4, 2, 512, TILE), BF16),
                pltpu.VMEM((4, 256, TILE), BF16),
                pltpu.VMEM((4, 128, 512), F32),
                pltpu.SMEM((4,), jnp.int32),
            ],
        ),
        out_shape=[jax.ShapeDtypeStruct((boxes, 128, targets), F32)] * 2,
        compiler_params=params(),
        name="leaf",
    )(info, *groups, circle, level_one, level_two, phase_one)

    pixel = jnp.asarray(pixel_matrix())
    image = image_part(info, partner, own, early_phase, phase_two, level_two, pixel, None, 0)
    image = image_part(info, partner, own, late_phase, phase_two, level_two, pixel, image, half)
    return image[None]


def solution(mesh):
    placed = (
        P(("quad", "box")),
        P(None, ("quad", "box")),
        P(None, ("quad", "box")),
        P(),
        P(),
        P("quad", "box", None, None),
        P("quad", "box", None, None),
    )
    return jax.shard_map(
        body, mesh=mesh, in_specs=placed, out_specs=P("quad", "box", None, None), check_vma=False
    )
```

time: 518 us -> 178 us (0.34); the launches traced: 509 us -> 179 us
  matrix products: 150 us -> 0 us
  waiting for transfers between devices: 175 us -> 40 us
  Pallas kernels: 0 us -> 111 us
  local copies, waits for them, and re-layouts: 96.4 us -> 6.55 us
  other arithmetic: 71.8 us -> 2.03 us
    dot_general x21 -> x0, matrix products: 150 us -> none  [the longest x8 59.7 us: leaf_block(): lax.dot_general(weights, real_part, dims, precision=lax.Precision.HIGHEST)]
    ppermute x2 -> x5, waiting for transfers between devices: 165 us -> 35.5 us  [from_quad(): return lax.ppermute(value, 'quad', pairs)]
    pallas_call x0 -> x5, Pallas kernels: none -> 111 us  [the longest x1 78.9 us: body(): pl.pallas_call(leaf_kernel, grid_spec=pltpu.PrefetchScalarGridSpec(num_sc...]
    add x33 -> x0, other arithmetic: 52.4 us -> none  [the longest x8 52.1 us: add_group(): running + leaf_block(block[0].astype(jnp.int32), block[1:5], block[5:7],...]
    gather x29 -> x0, local copies, waits for them, and re-layouts: 43.3 us -> none  [the longest x1 11.8 us: body(): sorted_owner = owner[order]]
    another operation x25 -> x2, local copies, waits for them, and re-layouts: 21 us -> 0.61 us  [body(): info = jnp.stack(starts + [bits], axis=0)]
    cos x2 -> x0, local copies, waits for them, and re-layouts: 16 us -> none  [rotate(): cosine = jnp.cos(angle)]
    mul x160 -> x0, local copies, waits for them, and re-layouts: 12.6 us -> none  [the longest x128 10.1 us: lagrange(): factor = factor * (points - nodes[other_node])]
  transfers between devices with their start and end apart: 3 -> 6, of which waited for: 3 -> 2; matrix products, arithmetic and copies ran while one was open for 3% -> 3% of each run, Pallas kernels for 0% -> 53%
where the time goes in v1:
time: 178 us; the launch traced here: 179 us
  Pallas kernels  111 us (62%)
  waiting for transfers between devices  40 us (22%)
  starting transfers between devices  18.9 us (11%)
  local copies, waits for them, and re-layouts  6.55 us (4%)
  other arithmetic  2.03 us (1%)
    pallas_call x1, Pallas kernels, body(): pl.pallas_call(leaf_kernel, grid_spec=pltpu.PrefetchScalarGridSpec(num_sc...  78.9 us
    ppermute x5, waiting for transfers between devices, from_quad(): return lax.ppermute(value, 'quad', pairs)  35.5 us
    pallas_call x2, Pallas kernels, image_part(): pl.pallas_call(image_kernel, grid_spec=pltpu.PrefetchScalarGridSpec(num_s...  20.2 us
    all_to_all x1, starting transfers between devices, body(): lax.all_to_all(packed.reshape(senders, 4, 128), 'box', split_axis=0, conc...  11.6 us
    ppermute x5, starting transfers between devices, from_quad(): return lax.ppermute(value, 'quad', pairs)  7.26 us
    pallas_call x1, Pallas kernels, body(): pl.pallas_call(sort_kernel, out_shape=jax.ShapeDtypeStruct((tiles + 3, 8,...  6.51 us
    pallas_call x1, Pallas kernels, body(): pl.pallas_call(pack_kernel, out_shape=jax.ShapeDtypeStruct((senders * 4,...  5.59 us
    all_to_all x1, waiting for transfers between devices, body(): lax.all_to_all(packed.reshape(senders, 4, 128), 'box', split_axis=0, conc...  4.58 us
  transfers between devices with their start and end apart: 6, of which 2 were waited for; matrix products, arithmetic and copies ran while one was open for 3% of the time, Pallas kernels for 53%

profile of v1, /device:TPU:67, one launch (start us, length us, event | category | flops | bytes accessed | tf_op | source)
XLA Modules:
  0.0 178.7 jit_solution(50988392591295365)
XLA Ops:
  0.0 5.6 %pack.1 = f32[256,128]{1,0:T(8,128)} custom-call(s32[1,2048]{1,0:T(1,128)} %bitcast.19, f32[4,2048]{1,0:T(4,128)} %coords_ref.1, f32[2,2048]{1,0:T(2,128)} %values_ref.1), custom_call_target="tpu_custom_call" | custom-call | tf_op jit(solution)/shard_map/pack/pallas_call | solution.py:337
  5.6 11.6 %all-to-all-start = ((f32[64,4,128]{2,1,0:T(4,128)}), f32[64,4,128]{2,1,0:T(4,128)S(1)}, u32[]{:S(2)}, u32[]{:S(2)}) async-start(f32[64,4,128]{2,1,0:T(4,128)} %bitcast.18), calls=%async_computation | async-start | bytes 262144 | tf_op jit(solution)/shard_map/all_to_all | solution.py:343
  17.2 2.7 %slice_bitcast_fusion = (f32[8,64,512]{2,1,0:T(8,128)}, f32[8,64,512]{2,1,0:T(8,128)S(1)}) fusion(f32[1,16,64,512]{3,2,1,0:T(8,128)} %param.18), kind=kLoop, calls=%fused_computation | loop fusion | bytes 4194304 | tf_op jit(solution)/shard_map/slice | solution.py:335
  20.0 1.8 %collective-permute-start.4 = (f32[8,64,512]{2,1,0:T(8,128)}, f32[8,64,512]{2,1,0:T(8,128)S(1)}, u32[]{:S(2)}, u32[]{:S(2)}) collective-permute-start(f32[8,64,512]{2,1,0:T(8,128)} %get-tuple-element.35), channel_id=1, source_target_pairs={{0,128},{64,192},{128,0},{192,64},{1,129},{65,193},{129,1},{193,65... | collective-permute-start | bytes 3145736 | tf_op jit(solution)/shard_map/ppermute | solution.py:290
  21.8 4.6 %all-to-all-done = f32[64,4,128]{2,1,0:T(4,128)S(1)} async-done(((f32[64,4,128]{2,1,0:T(4,128)}), f32[64,4,128]{2,1,0:T(4,128)S(1)}, u32[]{:S(2)}, u32[]{:S(2)}) %all-to-all-start) | async-done | bytes 131104 | tf_op jit(solution)/shard_map/all_to_all | solution.py:343
  26.4 0.6 copy-done.2
  27.0 6.5 %sort.1.s0_ref = f32[35,8,128]{2,1,0:T(8,128)} custom-call(f32[256,128]{1,0:T(8,128)} %bitcast.17), custom_call_target="tpu_custom_call" | custom-call | tf_op jit(solution)/shard_map/sort/pallas_call | solution.py:346
  33.6 1.8 %collective-permute-start.3 = (f32[8,64,512]{2,1,0:T(8,128)S(1)}, f32[8,64,512]{2,1,0:T(8,128)S(1)}, u32[]{:S(2)}, u32[]{:S(2)}) collective-permute-start(f32[8,64,512]{2,1,0:T(8,128)S(1)} %get-tuple-element.34), channel_id=1, source_target_pairs={{0,128},{64,192},{128,0},{192,64},{1,129},{65,193},{129,1},{193,65... | collective-permute-start | bytes 3145736 | tf_op jit(solution)/shard_map/ppermute | solution.py:290
  35.4 0.1 scatter.9
  35.5 3.0 %collective-permute-start.1 = (f32[35,8,128]{2,1,0:T(8,128)}, f32[35,8,128]{2,1,0:T(8,128)S(1)}, u32[]{:S(2)}, u32[]{:S(2)}) collective-permute-start(f32[35,8,128]{2,1,0:T(8,128)} %sort.1.s0_ref), channel_id=1, source_target_pairs={{0,128},{64,192},{128,0},{192,64},{1,129},{65,193},{129,1},{193,65... | collective-permute-start | bytes 430088 | tf_op jit(solution)/shard_map/ppermute | solution.py:290
  38.5 0.9 fusion.3
  39.4 0.6 collective-permute-start
  40.0 35.4 %collective-permute-done.2.s3_ref = f32[35,8,128]{2,1,0:T(8,128)S(1)} collective-permute-done((f32[35,8,128]{2,1,0:T(8,128)}, f32[35,8,128]{2,1,0:T(8,128)S(1)}, u32[]{:S(2)}, u32[]{:S(2)}) %collective-permute-start.2) | collective-permute-done | bytes 143392 | tf_op jit(solution)/shard_map/ppermute | solution.py:290
  75.5 0.1 fusion
  75.6 0.1 convert_element_type.59
  75.7 0.2 fusion.1
  75.9 0.1 convert_element_type.57
  76.0 0.9 fusion.2
  76.9 0.6 stack.14.info_ref
  77.5 78.9 %leaf.1 = (f32[16,128,512]{2,1,0:T(8,128)}, f32[16,128,512]{2,1,0:T(8,128)}) custom-call(s32[5,24]{1,0:T(8,128)} %stack.14.info_ref, f32[35,8,128]{2,1,0:T(8,128)} %sort.1.s0_ref, f32[35,8,128]{2,1,0:T(8,128)} %collective-permute-done.s1_ref, f32[35,8,128]{2,1,0:T(8,128)} %copy-done.4, f32[35,8,128]{2,1,0:T(8,128)} %copy-done.3, ...), custom_call_target="tpu_custom_call" | custom-call | tf_op jit(solution)/shard_map/leaf/pallas_call | solution.py:369
  156.4 1.0 copy-done
  157.4 10.1 %image_part.2.rest_0_ = f32[16,128,512]{2,1,0:T(8,128)} custom-call(s32[5,24]{1,0:T(8,128)} %stack.14.info_ref, f32[16,128,512]{2,1,0:T(8,128)} %get-tuple-element.32.partner_ref, f32[16,128,512]{2,1,0:T(8,128)} %get-tuple-element.33.own_ref, f32[8,64,512]{2,1,0:T(8,128)} %copy-done, f32[16,64,512]{2,1,0:T(8,128)} %bitcast.15, ...), custom_call_target="tpu_custom_call" | custom-call | tf_op jit(solution)/shard_map/image_part/pallas_call | solution.py:314
  167.5 1.0 copy-done.1
  168.6 10.1 %image_part.3 = f32[16,128,512]{2,1,0:T(8,128)} custom-call(s32[5,24]{1,0:T(8,128)} %stack.14.info_ref, f32[16,128,512]{2,1,0:T(8,128)} %get-tuple-element.32.partner_ref, f32[16,128,512]{2,1,0:T(8,128)} %get-tuple-element.33.own_ref, f32[8,64,512]{2,1,0:T(8,128)} %copy-done.1, f32[16,64,512]{2,1,0:T(8,128)} %bitcast.16, ...), custom_call_target="tpu_custom_call", output_to_operand_aliasing={{}: (7, {})} | custom-call | tf_op jit(solution)/shard_map/image_part/pallas_call | solution.py:314
  (15 shorter events, 0.2 us)
Async XLA Ops:
  5.6 20.8 %all-to-all-start = ((f32[64,4,128]{2,1,0:T(4,128)}), f32[64,4,128]{2,1,0:T(4,128)S(1)}, u32[]{:S(2)}, u32[]{:S(2)}) async-start(f32[64,4,128]{2,1,0:T(4,128)} %bitcast.18), calls=%async_computation | async-start | bytes 262144 | tf_op jit(solution)/shard_map/all_to_all | solution.py:343
  20.0 136.4 %collective-permute-start.4 = (f32[8,64,512]{2,1,0:T(8,128)}, f32[8,64,512]{2,1,0:T(8,128)S(1)}, u32[]{:S(2)}, u32[]{:S(2)}) collective-permute-start(f32[8,64,512]{2,1,0:T(8,128)} %get-tuple-element.35), channel_id=1, source_target_pairs={{0,128},{64,192},{128,0},{192,64},{1,129},{65,193},{129,1},{193,65... | collective-permute-start | bytes 3145736 | tf_op jit(solution)/shard_map/ppermute | solution.py:290
  26.4 0.6 copy-start.2
  33.6 134.0 %collective-permute-start.3 = (f32[8,64,512]{2,1,0:T(8,128)S(1)}, f32[8,64,512]{2,1,0:T(8,128)S(1)}, u32[]{:S(2)}, u32[]{:S(2)}) collective-permute-start(f32[8,64,512]{2,1,0:T(8,128)S(1)} %get-tuple-element.34), channel_id=1, source_target_pairs={{0,128},{64,192},{128,0},{192,64},{1,129},{65,193},{129,1},{193,65... | collective-permute-start | bytes 3145736 | tf_op jit(solution)/shard_map/ppermute | solution.py:290
  35.4 40.1 %collective-permute-start.2 = (f32[35,8,128]{2,1,0:T(8,128)}, f32[35,8,128]{2,1,0:T(8,128)S(1)}, u32[]{:S(2)}, u32[]{:S(2)}) collective-permute-start(f32[35,8,128]{2,1,0:T(8,128)} %sort.1.s0_ref), channel_id=1, source_target_pairs={{0,192},{64,128},{128,64},{192,0},{1,193},{65,129},{129,65},{193,1... | collective-permute-start | bytes 430088 | tf_op jit(solution)/shard_map/ppermute | solution.py:290
  35.5 40.2 %collective-permute-start.1 = (f32[35,8,128]{2,1,0:T(8,128)}, f32[35,8,128]{2,1,0:T(8,128)S(1)}, u32[]{:S(2)}, u32[]{:S(2)}) collective-permute-start(f32[35,8,128]{2,1,0:T(8,128)} %sort.1.s0_ref), channel_id=1, source_target_pairs={{0,128},{64,192},{128,0},{192,64},{1,129},{65,193},{129,1},{193,65... | collective-permute-start | bytes 430088 | tf_op jit(solution)/shard_map/ppermute | solution.py:290
  39.4 36.6 %collective-permute-start = (f32[35,8,128]{2,1,0:T(8,128)}, f32[35,8,128]{2,1,0:T(8,128)}, u32[]{:S(2)}, u32[]{:S(2)}) collective-permute-start(f32[35,8,128]{2,1,0:T(8,128)} %sort.1.s0_ref), channel_id=1, source_target_pairs={{0,64},{64,0},{128,192},{192,128},{1,65},{65,1},{129,193},{193,129... | collective-permute-start | bytes 430088 | tf_op jit(solution)/shard_map/ppermute | solution.py:290
  75.5 2.0 %copy-start.3 = (f32[35,8,128]{2,1,0:T(8,128)}, f32[35,8,128]{2,1,0:T(8,128)S(1)}, u32[]{:S(2)}) copy-start(f32[35,8,128]{2,1,0:T(8,128)S(1)} %collective-permute-done.2.s3_ref) | copy-start | bytes 430084
  75.7 1.8 %copy-start.4 = (f32[35,8,128]{2,1,0:T(8,128)}, f32[35,8,128]{2,1,0:T(8,128)S(1)}, u32[]{:S(2)}) copy-start(f32[35,8,128]{2,1,0:T(8,128)S(1)} %collective-permute-done.1.s2_ref) | copy-start | bytes 430084
  156.4 1.1 copy-start
  167.5 1.1 copy-start.1
